TPU v7x, 128 devices: a whole 4x4x4 slice. The times are simulated.
128 devices in a mesh: area: 8 (over x, core), sub: 16 (over z, y).
Axes of the slice: x: 4, y: 4, z: 4, core: 2. Of those that a mesh axis runs over, the one named last changes fastest.
Arguments:
- blocks: float32 [8, 1024, 64, 256], P('area', 'sub'), as said below
- pattern: int32 [8, 1024, 4], P('area', 'sub'), may hold values from 0 to 1023, as said below
- line_ends: int32 [8, 2, 64], P('area'), may hold values from 0 to 65535, as said below
- sources: float32 [4, 8, 65536], P(None, 'area', 'sub'), may hold values from -6 to 6
- capacity: float32 [8, 65536], P('area', 'sub'), may hold values from 0.2 to 2
- start_volt: float32 [8, 65536], P('area', 'sub'), may hold values from -6 to 6
- start_hist: float32 [8, 2, 64], P('area'), may hold values from -6 to 6
- surge: float32 [8, 64], P('area'), may hold values from 0.2 to 1
Outputs:
- volt: float32 [8, 65536], P('area', 'sub')
- hist: float32 [8, 2, 64], P('area')
Inputs may be any that keep to these rules, and one draw needn't show every extreme that they name: pattern[a, r, 0] = r. Split the 1024 block rows of an area into aligned groups of 64: the other entries of a row never point into the row's own group, no two of them in one group are equal, and the entries of one group point into between 12 and 13 distinct block rows of each other group, exactly 13 for some group. `line_ends`: within an area the line-end buses are distinct and rise from the first left end to the last right end. `blocks`: the diagonal of each first stored block lies in 2 to 4.
All inputs are finite; a program needn't handle non-finite values.
Results may differ from a plain program's by a relative error of at most 0.00011.
Values sent between devices are 32-bit elements; how exact they have to be, the bound alone decides.
A program may use at most 64 MiB of HBM per device.

v0:
```python
import jax
import jax.numpy as jnp
from jax import lax
from jax.sharding import PartitionSpec as P

STEPS = 4
SWEEPS = 8


def shifted(value, axis, steps):
    count = lax.axis_size(axis)
    pairs = [(source, (source + steps) % count) for source in range(count)]
    return lax.ppermute(value, axis, pairs)


def collect(field):
    return lax.all_gather(field, "sub", axis=1, tiled=True)


def apply_blocks(blocks, own_part, others):
    picked = jnp.concatenate([own_part, others], axis=1)
    result = jnp.einsum("rik,rk->ri", blocks[0], picked, precision=lax.Precision.HIGHEST)
    return result.reshape(1, -1)


def on_device(blocks, pattern, line_ends, sources, capacity, start_volt, start_hist, surge):
    width = blocks.shape[2]
    rows_here = blocks.shape[1]
    local_count = rows_here * width
    offset = lax.axis_index("sub") * local_count
    diag = jnp.diagonal(blocks[..., :width], axis1=2, axis2=3).reshape(1, local_count)
    system_diag = diag + capacity
    remote_cols = pattern[0][:, 1:].reshape(-1)
    local_ends = line_ends - offset
    inside = (local_ends >= 0) & (local_ends < local_count)
    safe_ends = jnp.clip(local_ends, 0, local_count - 1)
    volt = start_volt
    hist = start_hist
    carried = []
    for step in range(STEPS):
        rhs = sources[step] + capacity * volt
        inject = jnp.where(inside, -hist, 0.0)
        rhs = rhs.at[0, safe_ends.reshape(-1)].add(inject.reshape(-1))
        field = volt
        for sweep in range(SWEEPS):
            own_part = field.reshape(rows_here, width)
            whole = collect(field)
            others = whole.reshape(-1, width)[remote_cols]
            others = others.reshape(rows_here, -1)
            result = apply_blocks(blocks, own_part, others)
            field = field + (rhs - result - capacity * field) / system_diag
        volt = field
        partial_volt = jnp.where(inside, volt[0][safe_ends[0]][None], 0.0)
        end_volt = lax.psum(partial_volt, "sub")
        message = -2.0 * surge * end_volt[:, 1] - hist[:, 1]
        new_left = shifted(message, "area", 1)
        outgoing_ends = jnp.stack([end_volt[:, 0], hist[:, 0]], axis=1)
        from_right = shifted(outgoing_ends, "area", -1)
        new_right = -2.0 * surge * from_right[:, 0] - from_right[:, 1]
        hist = jnp.stack([new_left, new_right], axis=1)
    return (volt, hist)


def solution(mesh):
    in_specs = (
        P("area", "sub", None, None),
        P("area", "sub", None),
        P("area", None, None),
        P(None, "area", "sub"),
        P("area", "sub"),
        P("area", "sub"),
        P("area", None, None),
        P("area", None),
    )
    out_specs = (P("area", "sub"), P("area", None, None))
    return jax.shard_map(
        on_device, mesh=mesh, in_specs=in_specs, out_specs=out_specs, check_vma=False
    )
```

profile of v0, /device:TPU:1, one launch (start us, length us, event | category | flops | bytes accessed | tf_op | source)
XLA Modules:
  0.0 1189.9 jit_solution(17338477219462624346)
XLA Ops:
  2.0 20.8 %all_gather.96 = f32[1,65536]{1,0:T(1,128)S(1)} all-gather(f32[1,4096]{1,0:T(1,128)} %param.13), channel_id=1, replica_groups=mesh['area'=8,'sub'=16] {'sub'}, dimensions={1}, use_global_device_ids=true | all-gather | bytes 278528 | tf_op jit(solution)/shard_map/all_gather | solution.py:17
  40.3 17.4 %all_gather.97 = f32[1,65536]{1,0:T(1,128)S(1)} all-gather(f32[1,4096]{1,0:T(1,128)S(1)} %get-tuple-element.71), channel_id=1, replica_groups=mesh['area'=8,'sub'=16] {'sub'}, dimensions={1}, use_global_device_ids=true | all-gather | bytes 278528 | tf_op jit(solution)/shard_map/all_gather | solution.py:17
  60.1 5.7 fusion.60
  66.6 16.7 %all_gather.98 = f32[1,65536]{1,0:T(1,128)S(1)} all-gather(f32[1,4096]{1,0:T(1,128)S(1)} %get-tuple-element.69), channel_id=1, replica_groups=mesh['area'=8,'sub'=16] {'sub'}, dimensions={1}, use_global_device_ids=true | all-gather | bytes 278528 | tf_op jit(solution)/shard_map/all_gather | solution.py:17
  85.7 5.7 fusion.58
  92.2 17.1 %all_gather.99 = f32[1,65536]{1,0:T(1,128)S(1)} all-gather(f32[1,4096]{1,0:T(1,128)S(1)} %get-tuple-element.67), channel_id=1, replica_groups=mesh['area'=8,'sub'=16] {'sub'}, dimensions={1}, use_global_device_ids=true | all-gather | bytes 278528 | tf_op jit(solution)/shard_map/all_gather | solution.py:17
  111.7 5.7 fusion.56
  118.3 17.2 %all_gather.100 = f32[1,65536]{1,0:T(1,128)S(1)} all-gather(f32[1,4096]{1,0:T(1,128)S(1)} %get-tuple-element.65), channel_id=1, replica_groups=mesh['area'=8,'sub'=16] {'sub'}, dimensions={1}, use_global_device_ids=true | all-gather | bytes 278528 | tf_op jit(solution)/shard_map/all_gather | solution.py:17
  137.9 5.7 fusion.54
  144.4 17.2 %all_gather.101 = f32[1,65536]{1,0:T(1,128)S(1)} all-gather(f32[1,4096]{1,0:T(1,128)S(1)} %get-tuple-element.63), channel_id=1, replica_groups=mesh['area'=8,'sub'=16] {'sub'}, dimensions={1}, use_global_device_ids=true | all-gather | bytes 278528 | tf_op jit(solution)/shard_map/all_gather | solution.py:17
  164.0 5.7 fusion.52
  170.6 17.7 %all_gather.102 = f32[1,65536]{1,0:T(1,128)S(1)} all-gather(f32[1,4096]{1,0:T(1,128)S(1)} %get-tuple-element.61), channel_id=1, replica_groups=mesh['area'=8,'sub'=16] {'sub'}, dimensions={1}, use_global_device_ids=true | all-gather | bytes 278528 | tf_op jit(solution)/shard_map/all_gather | solution.py:17
  190.6 5.7 fusion.50
  197.2 16.4 %all_gather.103 = f32[1,65536]{1,0:T(1,128)S(1)} all-gather(f32[1,4096]{1,0:T(1,128)S(1)} %get-tuple-element.59), channel_id=1, replica_groups=mesh['area'=8,'sub'=16] {'sub'}, dimensions={1}, use_global_device_ids=true | all-gather | bytes 278528 | tf_op jit(solution)/shard_map/all_gather | solution.py:17
  216.0 5.7 fusion.48
  223.9 30.9 %psum.28 = f32[1,2,64]{2,1,0:T(2,128)S(1)} all-reduce(f32[1,2,64]{2,1,0:T(2,128)S(1)} %broadcast_select_fusion.3), channel_id=1, replica_groups=mesh['area'=8,'sub'=16] {'sub'}, use_global_device_ids=true, to_apply=%region_1.2 | all-reduce | flops 128 | bytes 1024 | tf_op jit(solution)/shard_map/psum | solution.py:54
  254.7 51.4 %collective-permute-start.1 = (f32[1,2,64]{2,1,0:T(2,128)S(1)}, f32[1,2,64]{2,1,0:T(2,128)S(1)}, u32[]{:S(2)}, u32[]{:S(2)}) collective-permute-start(f32[1,2,64]{2,1,0:T(2,128)S(1)} %pad_maximum_fusion), channel_id=1, source_target_pairs={{0,112},{16,0},{32,16},{48,32},{64,48},{80,64},{96,80},{112,96},{1... | collective-permute-start | bytes 1544 | tf_op jit(solution)/shard_map/ppermute | solution.py:13
  306.1 15.7 %all_gather.104 = f32[1,65536]{1,0:T(1,128)S(1)} all-gather(f32[1,4096]{1,0:T(1,128)S(1)} %get-tuple-element.53), channel_id=1, replica_groups=mesh['area'=8,'sub'=16] {'sub'}, dimensions={1}, use_global_device_ids=true | all-gather | bytes 278528 | tf_op jit(solution)/shard_map/all_gather | solution.py:17
  324.3 6.5 collective-permute-start
  338.9 18.3 %all_gather.105 = f32[1,65536]{1,0:T(1,128)S(1)} all-gather(f32[1,4096]{1,0:T(1,128)S(1)} %get-tuple-element.51), channel_id=1, replica_groups=mesh['area'=8,'sub'=16] {'sub'}, dimensions={1}, use_global_device_ids=true | all-gather | bytes 278528 | tf_op jit(solution)/shard_map/all_gather | solution.py:17
  359.6 5.7 fusion.44
  366.2 16.2 %all_gather.106 = f32[1,65536]{1,0:T(1,128)S(1)} all-gather(f32[1,4096]{1,0:T(1,128)S(1)} %get-tuple-element.49), channel_id=1, replica_groups=mesh['area'=8,'sub'=16] {'sub'}, dimensions={1}, use_global_device_ids=true | all-gather | bytes 278528 | tf_op jit(solution)/shard_map/all_gather | solution.py:17
  384.9 5.7 fusion.42
  391.5 17.8 %all_gather.107 = f32[1,65536]{1,0:T(1,128)S(1)} all-gather(f32[1,4096]{1,0:T(1,128)S(1)} %get-tuple-element.47), channel_id=1, replica_groups=mesh['area'=8,'sub'=16] {'sub'}, dimensions={1}, use_global_device_ids=true | all-gather | bytes 278528 | tf_op jit(solution)/shard_map/all_gather | solution.py:17
  411.8 5.7 fusion.40
  418.3 16.3 %all_gather.108 = f32[1,65536]{1,0:T(1,128)S(1)} all-gather(f32[1,4096]{1,0:T(1,128)S(1)} %get-tuple-element.45), channel_id=1, replica_groups=mesh['area'=8,'sub'=16] {'sub'}, dimensions={1}, use_global_device_ids=true | all-gather | bytes 278528 | tf_op jit(solution)/shard_map/all_gather | solution.py:17
  437.1 5.7 fusion.38
  443.7 17.6 %all_gather.109 = f32[1,65536]{1,0:T(1,128)S(1)} all-gather(f32[1,4096]{1,0:T(1,128)S(1)} %get-tuple-element.43), channel_id=1, replica_groups=mesh['area'=8,'sub'=16] {'sub'}, dimensions={1}, use_global_device_ids=true | all-gather | bytes 278528 | tf_op jit(solution)/shard_map/all_gather | solution.py:17
  463.7 5.7 fusion.36
  470.3 16.9 %all_gather.110 = f32[1,65536]{1,0:T(1,128)S(1)} all-gather(f32[1,4096]{1,0:T(1,128)S(1)} %get-tuple-element.41), channel_id=1, replica_groups=mesh['area'=8,'sub'=16] {'sub'}, dimensions={1}, use_global_device_ids=true | all-gather | bytes 278528 | tf_op jit(solution)/shard_map/all_gather | solution.py:17
  489.7 5.7 fusion.34
  496.2 17.5 %all_gather.111 = f32[1,65536]{1,0:T(1,128)S(1)} all-gather(f32[1,4096]{1,0:T(1,128)S(1)} %get-tuple-element.39), channel_id=1, replica_groups=mesh['area'=8,'sub'=16] {'sub'}, dimensions={1}, use_global_device_ids=true | all-gather | bytes 278528 | tf_op jit(solution)/shard_map/all_gather | solution.py:17
  516.2 5.7 fusion.32
  522.8 16.5 %all_gather.112 = f32[1,65536]{1,0:T(1,128)S(1)} all-gather(f32[1,4096]{1,0:T(1,128)S(1)} %get-tuple-element.35), channel_id=1, replica_groups=mesh['area'=8,'sub'=16] {'sub'}, dimensions={1}, use_global_device_ids=true | all-gather | bytes 278528 | tf_op jit(solution)/shard_map/all_gather | solution.py:17
  542.8 31.3 %psum.29 = f32[1,2,64]{2,1,0:T(2,128)S(1)} all-reduce(f32[1,2,64]{2,1,0:T(2,128)S(1)} %broadcast_select_fusion.2), channel_id=1, replica_groups=mesh['area'=8,'sub'=16] {'sub'}, use_global_device_ids=true, to_apply=%region_3.4 | all-reduce | flops 128 | bytes 1024 | tf_op jit(solution)/shard_map/psum | solution.py:54
  574.1 48.5 %collective-permute-start.3 = (f32[1,2,64]{2,1,0:T(2,128)S(1)}, f32[1,2,64]{2,1,0:T(2,128)S(1)}, u32[]{:S(2)}, u32[]{:S(2)}) collective-permute-start(f32[1,2,64]{2,1,0:T(2,128)S(1)} %pad_maximum_fusion.1), channel_id=1, source_target_pairs={{0,112},{16,0},{32,16},{48,32},{64,48},{80,64},{96,80},{112,96},{1... | collective-permute-start | bytes 1544 | tf_op jit(solution)/shard_map/ppermute | solution.py:13
  633.2 15.7 %all_gather.113 = f32[1,65536]{1,0:T(1,128)S(1)} all-gather(f32[1,4096]{1,0:T(1,128)S(1)} %get-tuple-element.33), channel_id=1, replica_groups=mesh['area'=8,'sub'=16] {'sub'}, dimensions={1}, use_global_device_ids=true | all-gather | bytes 278528 | tf_op jit(solution)/shard_map/all_gather | solution.py:17
  651.3 5.7 fusion.28
  657.9 18.1 %all_gather.114 = f32[1,65536]{1,0:T(1,128)S(1)} all-gather(f32[1,4096]{1,0:T(1,128)S(1)} %get-tuple-element.31), channel_id=1, replica_groups=mesh['area'=8,'sub'=16] {'sub'}, dimensions={1}, use_global_device_ids=true | all-gather | bytes 278528 | tf_op jit(solution)/shard_map/all_gather | solution.py:17
  678.5 5.7 fusion.26
  685.1 15.6 %all_gather.115 = f32[1,65536]{1,0:T(1,128)S(1)} all-gather(f32[1,4096]{1,0:T(1,128)S(1)} %get-tuple-element.29), channel_id=1, replica_groups=mesh['area'=8,'sub'=16] {'sub'}, dimensions={1}, use_global_device_ids=true | all-gather | bytes 278528 | tf_op jit(solution)/shard_map/all_gather | solution.py:17
  703.2 5.7 fusion.24
  709.8 18.2 %all_gather.116 = f32[1,65536]{1,0:T(1,128)S(1)} all-gather(f32[1,4096]{1,0:T(1,128)S(1)} %get-tuple-element.27), channel_id=1, replica_groups=mesh['area'=8,'sub'=16] {'sub'}, dimensions={1}, use_global_device_ids=true | all-gather | bytes 278528 | tf_op jit(solution)/shard_map/all_gather | solution.py:17
  730.4 5.7 fusion.22
  737.0 16.1 %all_gather.117 = f32[1,65536]{1,0:T(1,128)S(1)} all-gather(f32[1,4096]{1,0:T(1,128)S(1)} %get-tuple-element.25), channel_id=1, replica_groups=mesh['area'=8,'sub'=16] {'sub'}, dimensions={1}, use_global_device_ids=true | all-gather | bytes 278528 | tf_op jit(solution)/shard_map/all_gather | solution.py:17
  755.6 5.7 fusion.20
  762.1 18.1 %all_gather.118 = f32[1,65536]{1,0:T(1,128)S(1)} all-gather(f32[1,4096]{1,0:T(1,128)S(1)} %get-tuple-element.23), channel_id=1, replica_groups=mesh['area'=8,'sub'=16] {'sub'}, dimensions={1}, use_global_device_ids=true | all-gather | bytes 278528 | tf_op jit(solution)/shard_map/all_gather | solution.py:17
  782.7 5.7 fusion.18
  789.2 16.6 %all_gather.119 = f32[1,65536]{1,0:T(1,128)S(1)} all-gather(f32[1,4096]{1,0:T(1,128)S(1)} %get-tuple-element.21), channel_id=1, replica_groups=mesh['area'=8,'sub'=16] {'sub'}, dimensions={1}, use_global_device_ids=true | all-gather | bytes 278528 | tf_op jit(solution)/shard_map/all_gather | solution.py:17
  808.3 5.7 fusion.16
  814.8 17.1 %all_gather.120 = f32[1,65536]{1,0:T(1,128)S(1)} all-gather(f32[1,4096]{1,0:T(1,128)S(1)} %get-tuple-element.17), channel_id=1, replica_groups=mesh['area'=8,'sub'=16] {'sub'}, dimensions={1}, use_global_device_ids=true | all-gather | bytes 278528 | tf_op jit(solution)/shard_map/all_gather | solution.py:17
  835.4 31.0 %psum.30 = f32[1,2,64]{2,1,0:T(2,128)S(1)} all-reduce(f32[1,2,64]{2,1,0:T(2,128)S(1)} %broadcast_select_fusion.1), channel_id=1, replica_groups=mesh['area'=8,'sub'=16] {'sub'}, use_global_device_ids=true, to_apply=%region_5.6 | all-reduce | flops 128 | bytes 1024 | tf_op jit(solution)/shard_map/psum | solution.py:54
  866.5 51.6 %collective-permute-start.5 = (f32[1,2,64]{2,1,0:T(2,128)S(1)}, f32[1,2,64]{2,1,0:T(2,128)S(1)}, u32[]{:S(2)}, u32[]{:S(2)}) collective-permute-start(f32[1,2,64]{2,1,0:T(2,128)S(1)} %pad_maximum_fusion.2), channel_id=1, source_target_pairs={{0,112},{16,0},{32,16},{48,32},{64,48},{80,64},{96,80},{112,96},{1... | collective-permute-start | bytes 1544 | tf_op jit(solution)/shard_map/ppermute | solution.py:13
  928.4 15.7 %all_gather.121 = f32[1,65536]{1,0:T(1,128)S(1)} all-gather(f32[1,4096]{1,0:T(1,128)S(1)} %get-tuple-element.15), channel_id=1, replica_groups=mesh['area'=8,'sub'=16] {'sub'}, dimensions={1}, use_global_device_ids=true | all-gather | bytes 278528 | tf_op jit(solution)/shard_map/all_gather | solution.py:17
  946.5 5.7 fusion.12
  953.0 18.2 %all_gather.122 = f32[1,65536]{1,0:T(1,128)S(1)} all-gather(f32[1,4096]{1,0:T(1,128)S(1)} %get-tuple-element.13), channel_id=1, replica_groups=mesh['area'=8,'sub'=16] {'sub'}, dimensions={1}, use_global_device_ids=true | all-gather | bytes 278528 | tf_op jit(solution)/shard_map/all_gather | solution.py:17
  973.6 5.7 fusion.10
  980.1 15.6 %all_gather.123 = f32[1,65536]{1,0:T(1,128)S(1)} all-gather(f32[1,4096]{1,0:T(1,128)S(1)} %get-tuple-element.11), channel_id=1, replica_groups=mesh['area'=8,'sub'=16] {'sub'}, dimensions={1}, use_global_device_ids=true | all-gather | bytes 278528 | tf_op jit(solution)/shard_map/all_gather | solution.py:17
  1004.7 18.2 %all_gather.124 = f32[1,65536]{1,0:T(1,128)S(1)} all-gather(f32[1,4096]{1,0:T(1,128)S(1)} %get-tuple-element.9), channel_id=1, replica_groups=mesh['area'=8,'sub'=16] {'sub'}, dimensions={1}, use_global_device_ids=true | all-gather | bytes 278528 | tf_op jit(solution)/shard_map/all_gather | solution.py:17
  1031.8 16.2 %all_gather.125 = f32[1,65536]{1,0:T(1,128)S(1)} all-gather(f32[1,4096]{1,0:T(1,128)S(1)} %get-tuple-element.7), channel_id=1, replica_groups=mesh['area'=8,'sub'=16] {'sub'}, dimensions={1}, use_global_device_ids=true | all-gather | bytes 278528 | tf_op jit(solution)/shard_map/all_gather | solution.py:17
  1057.0 17.7 %all_gather.126 = f32[1,65536]{1,0:T(1,128)S(1)} all-gather(f32[1,4096]{1,0:T(1,128)S(1)} %get-tuple-element.5), channel_id=1, replica_groups=mesh['area'=8,'sub'=16] {'sub'}, dimensions={1}, use_global_device_ids=true | all-gather | bytes 278528 | tf_op jit(solution)/shard_map/all_gather | solution.py:17
  1083.6 16.9 %all_gather.127 = f32[1,65536]{1,0:T(1,128)S(1)} all-gather(f32[1,4096]{1,0:T(1,128)S(1)} %get-tuple-element.3), channel_id=1, replica_groups=mesh['area'=8,'sub'=16] {'sub'}, dimensions={1}, use_global_device_ids=true | all-gather | bytes 278528 | tf_op jit(solution)/shard_map/all_gather | solution.py:17
  1110.0 31.0 %psum.31 = f32[1,2,64]{2,1,0:T(2,128)S(1)} all-reduce(f32[1,2,64]{2,1,0:T(2,128)S(1)} %broadcast_select_fusion), channel_id=1, replica_groups=mesh['area'=8,'sub'=16] {'sub'}, use_global_device_ids=true, to_apply=%region_7.8 | all-reduce | flops 128 | bytes 1024 | tf_op jit(solution)/shard_map/psum | solution.py:54
  1141.0 44.5 %collective-permute-start.7 = (f32[1,2,64]{2,1,0:T(2,128)S(1)}, f32[1,2,64]{2,1,0:T(2,128)S(1)}, u32[]{:S(2)}, u32[]{:S(2)}) collective-permute-start(f32[1,2,64]{2,1,0:T(2,128)S(1)} %pad_maximum_fusion.3), channel_id=1, source_target_pairs={{0,112},{16,0},{32,16},{48,32},{64,48},{80,64},{96,80},{112,96},{1... | collective-permute-start | bytes 1544 | tf_op jit(solution)/shard_map/ppermute | solution.py:13
  (355 shorter events, 181.7 us)
Async XLA Ops:
  25.8 297.5 %copy-start.3 = (s32[1024]{0:T(1024)}, s32[1024]{0:T(1024)S(1)}, u32[]{:S(2)}) copy-start(s32[1024]{0:T(1024)S(1)} %pad_clamp_fusion.1) | copy-start | bytes 12292
  28.1 2.2 copy-start
  28.1 6.1 slice-start
  30.3 9.3 copy-start.2
  30.3 9.3 copy-start.5
  197.2 57.6 %slice-start.1 = ((f32[1,2,64]{2,1,0:T(2,128)}), f32[1,1,64]{2,1,0:T(1,128)S(1)}, s32[]{:S(2)}) async-start(f32[1,2,64]{2,1,0:T(2,128)} %param.14), calls=%async_computation.1 | async-start | bytes 1024 | tf_op jit(solution)/shard_map/slice | solution.py:57
  213.5 108.3 %copy-start.6 = (f32[4,1,4096]{2,1,0:T(1,128)S(1)}, f32[4,1,4096]{2,1,0:T(1,128)}, u32[]{:S(2)}) copy-start(f32[4,1,4096]{2,1,0:T(1,128)} %param.11) | copy-start | bytes 196612
  215.9 108.3 %copy-start.7 = (f32[1,64]{1,0:T(1,128)S(1)}, f32[1,64]{1,0:T(1,128)}, u32[]{:S(2)}) copy-start(f32[1,64]{1,0:T(1,128)} %param.15) | copy-start | bytes 772
  216.0 108.3 %copy-start.8 = (f32[1,2,64]{2,1,0:T(2,128)S(1)}, f32[1,2,64]{2,1,0:T(2,128)}, u32[]{:S(2)}) copy-start(f32[1,2,64]{2,1,0:T(2,128)} %param.14) | copy-start | bytes 1540
  254.7 69.5 %collective-permute-start.1 = (f32[1,2,64]{2,1,0:T(2,128)S(1)}, f32[1,2,64]{2,1,0:T(2,128)S(1)}, u32[]{:S(2)}, u32[]{:S(2)}) collective-permute-start(f32[1,2,64]{2,1,0:T(2,128)S(1)} %pad_maximum_fusion), channel_id=1, source_target_pairs={{0,112},{16,0},{32,16},{48,32},{64,48},{80,64},{96,80},{112,96},{1... | collective-permute-start | bytes 1544 | tf_op jit(solution)/shard_map/ppermute | solution.py:13
  324.3 12.3 %collective-permute-start = (f32[1,64]{1,0:T(1,128)S(1)}, f32[1,64]{1,0:T(1,128)S(1)}, u32[]{:S(2)}, u32[]{:S(2)}) collective-permute-start(f32[1,64]{1,0:T(1,128)S(1)} %get-tuple-element.84), channel_id=1, source_target_pairs={{0,16},{16,32},{32,48},{48,64},{64,80},{80,96},{96,112},{112,0},{1... | collective-permute-start | bytes 776 | tf_op jit(solution)/shard_map/ppermute | solution.py:13
  515.0 25.8 %copy-start.4 = (s32[1024]{0:T(1024)S(1)}, s32[1024]{0:T(1024)}, u32[]{:S(2)}) copy-start(s32[1024]{0:T(1024)} %copy-done.3) | copy-start | bytes 12292
  574.1 50.9 %collective-permute-start.3 = (f32[1,2,64]{2,1,0:T(2,128)S(1)}, f32[1,2,64]{2,1,0:T(2,128)S(1)}, u32[]{:S(2)}, u32[]{:S(2)}) collective-permute-start(f32[1,2,64]{2,1,0:T(2,128)S(1)} %pad_maximum_fusion.1), channel_id=1, source_target_pairs={{0,112},{16,0},{32,16},{48,32},{64,48},{80,64},{96,80},{112,96},{1... | collective-permute-start | bytes 1544 | tf_op jit(solution)/shard_map/ppermute | solution.py:13
  625.0 5.9 collective-permute-start.2
  866.5 53.8 %collective-permute-start.5 = (f32[1,2,64]{2,1,0:T(2,128)S(1)}, f32[1,2,64]{2,1,0:T(2,128)S(1)}, u32[]{:S(2)}, u32[]{:S(2)}) collective-permute-start(f32[1,2,64]{2,1,0:T(2,128)S(1)} %pad_maximum_fusion.2), channel_id=1, source_target_pairs={{0,112},{16,0},{32,16},{48,32},{64,48},{80,64},{96,80},{112,96},{1... | collective-permute-start | bytes 1544 | tf_op jit(solution)/shard_map/ppermute | solution.py:13
  920.3 5.9 collective-permute-start.4
  1108.7 80.6 %copy-start.1 = (f32[1,4096]{1,0:T(1,128)}, f32[1,4096]{1,0:T(1,128)S(1)}, u32[]{:S(2)}) copy-start(f32[1,4096]{1,0:T(1,128)S(1)} %divide_add_fusion) | copy-start | bytes 49156
  1141.0 46.7 %collective-permute-start.7 = (f32[1,2,64]{2,1,0:T(2,128)S(1)}, f32[1,2,64]{2,1,0:T(2,128)S(1)}, u32[]{:S(2)}, u32[]{:S(2)}) collective-permute-start(f32[1,2,64]{2,1,0:T(2,128)S(1)} %pad_maximum_fusion.3), channel_id=1, source_target_pairs={{0,112},{16,0},{32,16},{48,32},{64,48},{80,64},{96,80},{112,96},{1... | collective-permute-start | bytes 1544 | tf_op jit(solution)/shard_map/ppermute | solution.py:13
  1187.7 1.1 collective-permute-start.6
where the time goes:
time: 1200 us; the launch traced here: 1190 us
  blocking collectives  671 us (56%)
  starting transfers between devices  203 us (17%)
  matrix products  181 us (15%)
  other arithmetic  74.7 us (6%)
  local copies, waits for them, and re-layouts  49.7 us (4%)
    all_gather x32, blocking collectives, collect(): return lax.all_gather(field, 'sub', axis=1, tiled=True)  547 us
    ppermute x8, starting transfers between devices, shifted(): return lax.ppermute(value, axis, pairs)  203 us
    dot_general x32, matrix products, apply_blocks(): jnp.einsum('rik,rk->ri', blocks[0], picked, precision=lax.Precision.HIGHEST)  181 us
    psum x4, blocking collectives, on_device(): end_volt = lax.psum(partial_volt, 'sub')  124 us
    all_gather x32, other arithmetic, collect(): return lax.all_gather(field, 'sub', axis=1, tiled=True)  40.4 us
    gather x32, local copies, waits for them, and re-layouts, on_device(): others = whole.reshape(-1, width)[remote_cols]  24.2 us
  transfers between devices with their start and end apart: 8, of which 4 were waited for; matrix products, arithmetic and copies ran while one was open for 2% of the time, Pallas kernels for 0%

commit v1 on v0

v1 whole, which is shorter than its diff:
```python
import jax
import jax.numpy as jnp
from jax import lax
from jax.experimental import pallas as pl
from jax.experimental.pallas import tpu as pltpu
from jax.sharding import PartitionSpec as P

STEPS = 4
SWEEPS = 8
MESH = pl.DeviceIdType.MESH
SIDE = 4
SUBS = 16
ROWS = 64
WIDTH = 64
LANES = 128
SLOTS = 16
TILES = 8


def ring_distance(offset):
    return sum(min(part, SIDE - part) for part in divmod(offset, SIDE))


OFFSETS = sorted(range(1, SUBS), key=lambda offset: -ring_distance(offset))


def negated(offset):
    along_z, along_y = divmod(offset, SIDE)
    return (-along_z % SIDE) * SIDE + -along_y % SIDE


def lane_gather(values, index):
    return jnp.take_along_axis(values, index, axis=1, mode="promise_in_bounds")


def iota(axis, rows=8, columns=LANES):
    return lax.broadcasted_iota(jnp.int32, (rows, columns), axis)


def row_total(tile):
    for shift in (4, 2, 1):
        tile = tile + pltpu.roll(tile, shift, 0)
    return tile


def xor_mix(tiles):
    chunk = iota(1) // SLOTS
    for bit in (1, 2, 4):
        mask = (chunk & bit) != 0
        tiles = [jnp.where(mask, tiles[d ^ bit], tiles[d]) for d in range(TILES)]
    return tiles


def fold_rows(tiles):
    sub = iota(0)
    first = []
    for s in range(4):
        low = sub < 4
        kept = jnp.where(low, tiles[s], tiles[s + 4])
        moved = jnp.where(low, tiles[s + 4], tiles[s])
        first.append(kept + pltpu.roll(moved, 4, 0))
    low = (sub & 2) == 0
    second = [
        jnp.where(low, first[s] + pltpu.roll(first[s], 6, 0), first[s + 2] + pltpu.roll(first[s + 2], 2, 0))
        for s in range(2)
    ]
    low = (sub & 1) == 0
    return jnp.where(low, second[0] + pltpu.roll(second[0], 7, 0), second[1] + pltpu.roll(second[1], 1, 0))


def nt_dot(left, right, precision=None):
    return lax.dot_general(
        left, right, (((1,), (1,)), ((), ())), precision=precision, preferred_element_type=jnp.float32
    )


def nn_dot(left, right):
    return jnp.dot(left, right, preferred_element_type=jnp.float32)


def kernel(
    blocks, ints, vecs, lines, volt_out, hist_out,
    stage, turned, own, xs, ys, rhs, inverse, diag, hist_s, index, places,
    list_snd, list_rcv, snd, rcv, line_snd, line_rcv,
    stage_sem, list_ss, list_rs, ss, rs, line_ss, line_rs,
):
    area = lax.axis_index("area")
    areas = lax.axis_size("area")
    me = lax.axis_index("sub")
    my_z, my_y = me // SIDE, me % SIDE

    def peer(offset):
        along_z, along_y = divmod(offset, SIDE)
        return {"sub": ((my_z + along_z) % SIDE) * SIDE + (my_y + along_y) % SIDE}

    peers = {offset: peer(offset) for offset in OFFSETS}
    line_peers = ({"area": (area + 1) % areas}, {"area": (area + areas - 1) % areas})

    stage_copies = [
        pltpu.make_async_copy(blocks.at[:, pl.ds(LANES * half, LANES)], stage.at[half], stage_sem.at[half])
        for half in range(2)
    ]
    for copy in stage_copies:
        copy.start()

    barrier = pltpu.get_barrier_semaphore()
    for target in (*peers.values(), *line_peers):
        pl.semaphore_signal(barrier, inc=1, device_id=target, device_id_type=MESH)

    lane = iota(1)
    sub = iota(0)
    low_half = lane < WIDTH
    slot = lane % SLOTS

    pattern = [ints[0:1, :], ints[1:2, :]]
    groups = [p >> 6 for p in pattern]
    locals_ = [p & 63 for p in pattern]
    group_hot = [jnp.where(iota(0, LANES) == g, 1.0, 0.0) for g in groups]
    local_hot = [jnp.where(iota(0, ROWS) == l, 1.0, 0.0) for l in locals_]
    used = nt_dot(local_hot[0], group_hot[0]) + nt_dot(local_hot[1], group_hot[1])
    used = used > 0.5
    before = jnp.where(iota(1, ROWS, ROWS) < iota(0, ROWS, ROWS), 1.0, 0.0)
    rank = nn_dot(before, jnp.where(used, 1.0, 0.0))
    rank = jnp.where(used, rank, 99.0)
    spread = jnp.where(iota(0, LANES, 2 * LANES) == iota(1, LANES, 2 * LANES) // SLOTS, 1.0, 0.0)
    spread_rank = nn_dot(rank, spread)
    wanted = (iota(1, ROWS, 2 * LANES) % SLOTS).astype(jnp.float32)
    lists = jnp.sum(
        jnp.where(spread_rank == wanted, iota(0, ROWS, 2 * LANES).astype(jnp.float32), 0.0), axis=0, keepdims=True
    )
    list_snd[...] = jnp.where(
        sub < 4, jnp.broadcast_to(lists[:, :LANES], (8, LANES)), jnp.broadcast_to(lists[:, LANES:], (8, LANES))
    )

    pl.semaphore_wait(barrier, len(OFFSETS) + 2)

    for offset in OFFSETS:
        pltpu.make_async_remote_copy(
            src_ref=list_snd, dst_ref=list_rcv.at[offset], send_sem=list_ss, recv_sem=list_rs,
            device_id=peers[offset], device_id_type=MESH,
        ).start()

    for half in range(2):
        ranks = nn_dot(rank, group_hot[half])
        own_slot = jnp.sum(local_hot[half] * ranks, axis=0, keepdims=True).astype(jnp.int32)
        along_z = (my_z - (groups[half] >> 2) + SIDE) & 3
        along_y = (my_y - (groups[half] & 3) + SIDE) & 3
        offset = along_z * SIDE + along_y
        place = (offset & 7) * SLOTS + own_slot
        places[2 * half] = jnp.broadcast_to(place, (8, LANES))
        places[2 * half + 1] = jnp.broadcast_to(offset >> 3, (8, LANES))

    for tile in range(TILES):
        xs[tile] = vecs[STEPS + 1, pl.ds(8 * tile, 8), :]
    hist_s[...] = jnp.broadcast_to(lines[0:1, :], (8, LANES))
    list_all = pltpu.make_async_remote_copy(
        src_ref=list_rcv.at[pl.ds(1, SUBS - 1)], dst_ref=list_rcv.at[pl.ds(1, SUBS - 1)],
        send_sem=list_ss, recv_sem=list_rs, device_id=peers[1], device_id_type=MESH,
    )
    list_all.wait_recv()
    list_all.wait_send()
    bases = [jnp.zeros((8, LANES), jnp.int32) for _ in range(2)]
    my_chunk = (me % 8) * SLOTS + slot
    for offset in OFFSETS:
        to = negated(offset)
        row = list_rcv[offset, pl.ds((me // 8) * 4, 1), :]
        row = lane_gather(jnp.broadcast_to(row, (8, LANES)), my_chunk).astype(jnp.int32)
        bases[to // 8] = jnp.where(lane // SLOTS == to % 8, row, bases[to // 8])
    for tile in range(TILES):
        for high in range(2):
            index[2 * tile + high] = lane_gather(bases[high], lane ^ (tile * SLOTS))

    bus = ints[2:3, :] - me * (ROWS * WIDTH)
    inside = (bus >= 0) & (bus < ROWS * WIDTH)
    end_row = jnp.where(inside, bus >> 6, 0)
    end_at = jnp.where(inside, bus & 63, -1)

    def end_volts(x):
        total = jnp.zeros((8, LANES), jnp.float32)
        rows_of = jnp.broadcast_to(end_row, (8, LANES))
        for tile in range(TILES):
            total = total + jnp.where(sub + 8 * tile == end_at, lane_gather(x[tile], rows_of), 0.0)
        return row_total(total)

    def injection(hist):
        ends = jnp.where(iota(0, WIDTH) == end_at, jnp.broadcast_to(hist[0:1], (WIDTH, LANES)), 0.0)
        rows_hot = jnp.where((iota(0, LANES) % ROWS) == end_row, 1.0, 0.0)
        return nt_dot(ends, rows_hot, lax.Precision.HIGHEST)

    def send(q, x, end_tile=None):
        for high in range(2):
            mixed = xor_mix([lane_gather(x[tile], index[2 * tile + high]) for tile in range(TILES)])
            for d in range(TILES):
                if high * 8 + d:
                    out = mixed[d] if end_tile is None else jnp.where(slot >= 13, end_tile, mixed[d])
                    snd[q, high * 8 + d] = out
        for offset in OFFSETS:
            pltpu.make_async_remote_copy(
                src_ref=snd.at[q, offset], dst_ref=rcv.at[q, offset], send_sem=ss.at[q], recv_sem=rs.at[q],
                device_id=peers[offset], device_id_type=MESH,
            ).start()

    def arrived(q):
        everything = pltpu.make_async_remote_copy(
            src_ref=snd.at[q, pl.ds(1, SUBS - 1)], dst_ref=rcv.at[q, pl.ds(1, SUBS - 1)],
            send_sem=ss.at[q], recv_sem=rs.at[q], device_id=peers[1], device_id_type=MESH,
        )
        everything.wait_recv()
        everything.wait_send()

    def own_part(x):
        parts = [jnp.where(low_half, x[p], x[p + 4]) for p in range(4)]
        for i in range(WIDTH):
            total = turned[i, 12] * parts[0]
            for p in range(1, 4):
                total = total + turned[i, 12 + p] * parts[p]
            own[i] = total

    def remote_part(q):
        mixed = []
        for high in range(2):
            mixed.append(xor_mix([rcv[q, max(1, 8 * high + d)] for d in range(TILES)]))
        place, high = places[0], places[1] != 0
        picked = []
        for tile in range(TILES):
            at = place ^ (tile * SLOTS)
            picked.append(jnp.where(high, lane_gather(mixed[1][tile], at), lane_gather(mixed[0][tile], at)))
        place, high = places[2], places[3] != 0
        for tile in range(4):
            at = [place ^ ((tile + 4 * h) * SLOTS) for h in range(2)]
            both = [
                jnp.where(high, lane_gather(mixed[1][tile + 4 * h], at[h]), lane_gather(mixed[0][tile + 4 * h], at[h]))
                for h in range(2)
            ]
            picked.append(jnp.where(low_half, both[0], both[1]))
        for tile in range(TILES):
            totals = []
            for s in range(8):
                i = tile * 8 + s
                total = own[i]
                for p in range(12):
                    total = total + turned[i, p] * picked[p]
                totals.append(total)
            folded = fold_rows(totals)
            ys[tile] = folded + pltpu.roll(folded, WIDTH, 1)

    def capacity(tile):
        return vecs[STEPS, pl.ds(8 * tile, 8), :]

    send(1, [xs[tile] for tile in range(TILES)])

    for copy in stage_copies:
        copy.wait()

    def turn(i, carry):
        rows = [stage[half, pl.ds(i, ROWS, stride=WIDTH), :] for half in range(2)]
        out = jnp.concatenate(rows, axis=0).T
        tiles = [out[8 * p : 8 * p + 8] for p in range(16)]
        for p in range(8):
            turned[i, p] = tiles[8 + p]
        for p in range(4):
            a, b = tiles[p], tiles[p + 4]
            turned[i, 8 + p] = jnp.where(low_half, pltpu.roll(a, WIDTH, 1), b)
            turned[i, 12 + p] = jnp.where(low_half, a, pltpu.roll(b, WIDTH, 1))
        return carry

    lax.fori_loop(0, WIDTH, turn, 0)
    for tile in range(TILES):
        at = jnp.zeros((8, LANES), jnp.float32)
        for s in range(8):
            at = jnp.where(sub == s, turned[8 * tile + s, 12 + tile % 4], at)
        other = pltpu.roll(at, WIDTH, 1)
        diagonal = jnp.where(low_half, at, other) if tile < 4 else jnp.where(low_half, other, at)
        inverse[tile] = 1.0 / (diagonal + capacity(tile))

    own_part([xs[tile] for tile in range(TILES)])
    arrived(1)
    remote_part(1)

    def update():
        x = []
        for tile in range(TILES):
            old = xs[tile]
            new = old + (rhs[tile] - ys[tile] - capacity(tile) * old) * inverse[tile]
            xs[tile] = new
            x.append(new)
        return x

    end_index = sub * SLOTS + (lane // SLOTS) * 2 + jnp.clip(slot - 13, 0, 1)
    end_back = ((lane % SLOTS) // 2) * SLOTS + 13 + lane % 2
    surge = jnp.broadcast_to(lines[1:2, :], (8, LANES))

    def step(t, carry):
        hist = hist_s[...]
        inject = injection(hist)
        for tile in range(TILES):
            rhs[tile] = vecs[t, pl.ds(8 * tile, 8), :] + capacity(tile) * xs[tile] - inject[8 * tile : 8 * tile + 8]

        def sweep(s, inner):
            q = s % 2
            x = update()
            send(q, x)
            own_part(x)
            arrived(q)
            remote_part(q)
            return inner

        lax.fori_loop(0, SWEEPS - 1, sweep, 0)
        q = (SWEEPS - 1) % 2
        tq = t % 2
        x = update()
        end_tile = lane_gather(end_volts(x), end_index)
        send(q, x, end_tile)
        own_part(x)
        arrived(q)
        total = end_tile
        for offset in range(1, SUBS):
            total = total + rcv[q, offset]
        total = jnp.where(sub == lane // SLOTS, lane_gather(total, end_back), 0.0)
        ends = row_total(total)
        hist = hist_s[...]
        line_snd[tq, 0] = -2.0 * surge * ends - hist
        line_snd[tq, 1] = jnp.where(low_half, ends, pltpu.roll(hist, WIDTH, 1))
        copies = [
            pltpu.make_async_remote_copy(
                src_ref=line_snd.at[tq, way], dst_ref=line_rcv.at[tq, way],
                send_sem=line_ss.at[tq, way], recv_sem=line_rs.at[tq, way],
                device_id=line_peers[way], device_id_type=MESH,
            )
            for way in range(2)
        ]
        for copy in copies:
            copy.start()
        remote_part(q)
        for copy in copies:
            copy.wait()
        from_left, from_right = line_rcv[tq, 0], line_rcv[tq, 1]
        hist_s[...] = jnp.where(
            low_half, pltpu.roll(from_left, WIDTH, 1), -2.0 * surge * pltpu.roll(from_right, WIDTH, 1) - from_right
        )
        return carry

    lax.fori_loop(0, STEPS, step, 0)
    volt = jnp.concatenate([xs[tile] for tile in range(TILES)], axis=0)
    volt_out[...] = jnp.concatenate([volt, volt], axis=0).T[:ROWS, :WIDTH]
    hist_out[...] = hist_s[...]


def on_device(blocks, pattern, line_ends, sources, capacity, start_volt, start_hist, surge):
    vectors = jnp.concatenate([sources[:, 0], capacity, start_volt], axis=0).reshape(STEPS + 2, ROWS, WIDTH)
    vectors = jnp.swapaxes(vectors, 1, 2)
    vectors = jnp.concatenate([vectors, vectors], axis=2)
    columns = pattern[0].T
    ints = jnp.stack(
        [
            jnp.concatenate([columns[1], columns[3]]),
            jnp.concatenate([columns[2], columns[2]]),
            line_ends.reshape(LANES),
        ]
    )
    lines = jnp.stack([start_hist.reshape(LANES), jnp.concatenate([surge[0], surge[0]])])
    tile = (8, LANES)
    f32 = jnp.float32
    vmem = pl.BlockSpec(memory_space=pltpu.VMEM)
    volt, hist = pl.pallas_call(
        kernel,
        out_shape=(jax.ShapeDtypeStruct((ROWS, WIDTH), f32), jax.ShapeDtypeStruct(tile, f32)),
        in_specs=[pl.BlockSpec(memory_space=pl.ANY), vmem, vmem, vmem],
        out_specs=(vmem, vmem),
        scratch_shapes=[
            pltpu.VMEM((2, ROWS * WIDTH, LANES), f32),
            pltpu.VMEM((WIDTH, 16, *tile), f32),
            pltpu.VMEM((WIDTH, *tile), f32),
            pltpu.VMEM((TILES, *tile), f32),
            pltpu.VMEM((TILES, *tile), f32),
            pltpu.VMEM((TILES, *tile), f32),
            pltpu.VMEM((TILES, *tile), f32),
            pltpu.VMEM((TILES, *tile), f32),
            pltpu.VMEM(tile, f32),
            pltpu.VMEM((2 * TILES, *tile), jnp.int32),
            pltpu.VMEM((4, *tile), jnp.int32),
            pltpu.VMEM(tile, f32),
            pltpu.VMEM((SUBS, *tile), f32),
            pltpu.VMEM((2, SUBS, *tile), f32),
            pltpu.VMEM((2, SUBS, *tile), f32),
            pltpu.VMEM((2, 2, *tile), f32),
            pltpu.VMEM((2, 2, *tile), f32),
            pltpu.SemaphoreType.DMA((2,)),
            pltpu.SemaphoreType.DMA,
            pltpu.SemaphoreType.DMA,
            pltpu.SemaphoreType.DMA((2,)),
            pltpu.SemaphoreType.DMA((2,)),
            pltpu.SemaphoreType.DMA((2, 2)),
            pltpu.SemaphoreType.DMA((2, 2)),
        ],
        compiler_params=pltpu.CompilerParams(
            collective_id=0, has_side_effects=True, vmem_limit_bytes=32 * 2**20
        ),
    )(blocks.reshape(ROWS * WIDTH, 4 * WIDTH), ints, vectors, lines)
    return volt.reshape(1, ROWS * WIDTH), hist[0].reshape(1, 2, WIDTH)


def solution(mesh):
    in_specs = (
        P("area", "sub", None, None),
        P("area", "sub", None),
        P("area", None, None),
        P(None, "area", "sub"),
        P("area", "sub"),
        P("area", "sub"),
        P("area", None, None),
        P("area", None),
    )
    out_specs = (P("area", "sub"), P("area", None, None))
    return jax.shard_map(
        on_device, mesh=mesh, in_specs=in_specs, out_specs=out_specs, check_vma=False
    )
```

time: 1200 us -> 209 us (0.17)
  blocking collectives: 671 us -> 0 us
  starting transfers between devices: 203 us -> 0 us
  Pallas kernels: 0 us -> 196 us
  matrix products: 181 us -> 0 us
  other arithmetic: 74.7 us -> 4.88 us
  local copies, waits for them, and re-layouts: 49.7 us -> 6.88 us
    all_gather x32 -> x0, blocking collectives: 547 us -> none  [collect(): return lax.all_gather(field, 'sub', axis=1, tiled=True)]
    ppermute x8 -> x0, starting transfers between devices: 203 us -> none  [shifted(): return lax.ppermute(value, axis, pairs)]
    pallas_call x0 -> x1, Pallas kernels: none -> 196 us  [on_device(): pl.pallas_call(kernel, out_shape=(jax.ShapeDtypeStruct((ROWS, WIDTH), f32...]
    dot_general x32 -> x0, matrix products: 181 us -> none  [apply_blocks(): jnp.einsum('rik,rk->ri', blocks[0], picked, precision=lax.Precision.HIGHEST)]
    psum x4 -> x0, blocking collectives: 124 us -> none  [on_device(): end_volt = lax.psum(partial_volt, 'sub')]
    all_gather x32 -> x0, other arithmetic: 40.4 us -> none  [collect(): return lax.all_gather(field, 'sub', axis=1, tiled=True)]
    gather x38 -> x0, local copies, waits for them, and re-layouts: 30.4 us -> none  [the longest x32 24.2 us: on_device(): others = whole.reshape(-1, width)[remote_cols]]
    add x36 -> x0, other arithmetic: 23.9 us -> none  [the longest x32 22.3 us: on_device(): field = field + (rhs - result - capacity * field) / system_diag]
  transfers between devices with their start and end apart: 8 -> 0, of which waited for: 4 -> 0; matrix products, arithmetic and copies ran while one was open for 2% -> 0% of each run, Pallas kernels for 0% -> 0%
where the time goes in v1:
time: 209 us; the launch traced here: 208 us
  Pallas kernels  196 us (94%)
  local copies, waits for them, and re-layouts  6.88 us (3%)
  other arithmetic  4.88 us (2%)
    pallas_call x1, Pallas kernels, on_device(): pl.pallas_call(kernel, out_shape=(jax.ShapeDtypeStruct((ROWS, WIDTH), f32...  196 us

profile of v1, /device:TPU:1, one launch (start us, length us, event | category | flops | bytes accessed | tf_op | source)
XLA Modules:
  0.0 208.3 jit_solution(17049581972838144760)
XLA Ops:
  0.6 0.8 slice_bitcast_fusion.2
  1.4 0.1 add_bitcast_fusion
  1.5 0.8 stack_reshape.6
  2.3 0.5 broadcast.10
  2.8 1.4 reduce.12
  4.2 0.1 concatenate.25
  4.3 0.1 copy.11
  4.3 1.4 reduce.11
  5.8 0.1 concatenate.26
  5.8 0.1 copy.12
  5.9 1.0 reduce
  6.9 0.1 concatenate.24
  7.1 0.1 copy.10
  7.2 0.1 pad_maximum_fusion.vecs
  7.3 0.8 maximum_bitcast_fusion.1
  8.1 0.8 stack_reshape.7
  8.9 0.0 copy-start
  8.9 2.2 %copy-done = f32[1,64,64,256]{3,2,1,0:T(8,128)S(1)} copy-done((f32[1,64,64,256]{3,2,1,0:T(8,128)S(1)}, f32[1,64,64,256]{3,2,1,0:T(8,128)}, u32[]{:S(2)}) %copy-start) | copy-done | bytes 4194328
  11.1 195.8 %shard_map.95 = (f32[64,64]{1,0:T(8,128)S(1)}, f32[8,128]{1,0:T(8,128)S(1)}) custom-call(f32[4096,256]{1,0:T(8,128)S(1)} %bitcast.19, s32[3,128]{1,0:T(4,128)S(1)} %pad_add_fusion.ints, f32[6,64,128]{2,1,0:T(8,128)S(1)} %pad_maximum_fusion.vecs, f32[2,128]{1,0:T(2,128)S(1)} %pad_maximum_fusion.1.lines), custom_call_target="tpu_custom_call" | custom-call | tf_op jit(solution)/shard_map/pallas_call | solution.py:365
  206.9 0.7 reshape.16
  207.6 0.6 reshape_squeeze.3
  (4 shorter events, 0.1 us)
Async XLA Ops:
  8.9 2.2 %copy-start = (f32[1,64,64,256]{3,2,1,0:T(8,128)S(1)}, f32[1,64,64,256]{3,2,1,0:T(8,128)}, u32[]{:S(2)}) copy-start(f32[1,64,64,256]{3,2,1,0:T(8,128)} %param.8) | copy-start | bytes 12582916
